TPU v7x, 256 devices: a whole 4x4x8 slice. The times are simulated.
256 devices in a mesh: grp: 4 (over x), dev: 64 (over z, y, core).
Axes of the slice: x: 4, y: 4, z: 8, core: 2. Of those that a mesh axis runs over, the one named last changes fastest.
Arguments:
- design: float32 [524288, 256], P(('grp', 'dev')), may hold values from -6 to 6
- sign_bits: int32 [524288], P(('grp', 'dev')), may hold values from 0 to 1
- sample_rows: int32 [4, 8192], P('grp'), may hold values from 0 to 131071, as said below
Outputs:
- sketch_rows: float32 [32768, 256], P(('grp', 'dev'))
- gram: float32 [256, 256], replicated
Inputs may be any that keep to these rules, and one draw needn't show every extreme that they name: `sample_rows`: split each slab's samples into 64 blocks of 128 in order, and the rows r of a slab into 64 ranges by (r % 2048) // 32. In every block each range holds either exactly 4 samples or none; rows may repeat.
All inputs are finite; a program needn't handle non-finite values.
Results may differ from a plain program's by a relative error of at most 0.0001.
Values sent between devices are 32-bit elements; how exact they have to be, the bound alone decides.
A program may use at most 64 MiB of HBM per device.

v0:
```python
import math

import jax
import jax.numpy as jnp
from jax import lax
from jax.sharding import PartitionSpec as P


def walsh_table(length):
    row_ids = jnp.arange(length, dtype=jnp.int32)[:, None]
    col_ids = jnp.arange(length, dtype=jnp.int32)[None, :]
    parity = jnp.zeros((length, length), jnp.int32)
    for level in range(length.bit_length() - 1):
        both = jnp.bitwise_and(jnp.right_shift(row_ids, level), 1) * jnp.bitwise_and(
            jnp.right_shift(col_ids, level), 1
        )
        parity = jnp.bitwise_xor(parity, both)
    return (1 - 2 * parity).astype(jnp.float32)


def shards(design, sign_bits, sample_rows):
    rows_dev, width = design.shape
    devices = lax.axis_size("dev")
    groups = lax.axis_size("grp")
    my_index = lax.axis_index("dev")
    slab = rows_dev * devices
    range_rows = rows_dev // devices
    samples = sample_rows.shape[1]
    scale = 1.0 / math.sqrt(slab)
    signed = design * (2 * sign_bits - 1).astype(jnp.float32)[:, None]
    local = jnp.dot(
        walsh_table(rows_dev),
        signed,
        precision=lax.Precision.HIGHEST,
        preferred_element_type=jnp.float32,
    )
    outer_table = walsh_table(devices)
    owned = (
        jnp.einsum(
            "de,ebc->dbc",
            outer_table,
            lax.all_to_all(
                local.reshape(devices, range_rows, width),
                "dev",
                split_axis=0,
                concat_axis=0,
                tiled=True,
            ),
            precision=lax.Precision.HIGHEST,
        )
        * scale
    )
    owned_flat = owned.reshape(devices * range_rows, width)
    targets = sample_rows[0]
    low_part = targets % rows_dev
    owner = low_part // range_rows
    place = targets // rows_dev * range_rows + low_part % range_rows
    mine = owner == my_index
    picked = jnp.take(owned_flat, place, axis=0)
    sketch = lax.psum_scatter(
        jnp.where(mine[:, None], picked, 0.0), "dev", scatter_dimension=0, tiled=True
    )
    partial_gram = jnp.dot(
        sketch.T, sketch, precision=lax.Precision.HIGHEST, preferred_element_type=jnp.float32
    )
    gram = lax.psum(partial_gram, ("grp", "dev")) / float(groups * samples)
    return (sketch, gram)


def solution(mesh):
    return jax.shard_map(
        shards,
        mesh=mesh,
        in_specs=(P(("grp", "dev"), None), P(("grp", "dev")), P("grp", None)),
        out_specs=(P(("grp", "dev"), None), P()),
        check_vma=False,
    )
```

profile of v0, /device:TPU:1, one launch (start us, length us, event | category | flops | bytes accessed | tf_op | source)
XLA Modules:
  0.0 556.0 jit_solution(9325756614432756214)
XLA Ops:
  7.2 0.7 add_convert_fusion
  7.9 1.9 fusion.107
  9.9 0.0 copy-start
  9.9 28.0 %fusion = f32[2048,256]{1,0:T(8,128)} fusion(s32[2048]{0:T(1024)S(1)} %get-tuple-element.5, s32[2048]{0:T(1024)S(1)} %get-tuple-element.6, s32[2048]{0:T(1024)S(1)} %get-tuple-element.7, s32[2048]{0:T(1024)S(1)} %get-tuple-element.8, s32[2048]{0:T(1024)S(1)} %get-tuple-element.9, s32[2048]{0:T(1024)S(1)} %get-tuple-element.10, ...), kind=kOutput, calls=%fused_computation.1 | convolution fusion | flops 12985565184 | bytes 4284416 | tf_op jit(solution)/shard_map/dot_general | solution.py:31
  37.8 13.2 %all-to-all-start = ((f32[64,32,256]{2,1,0:T(8,128)}), f32[64,32,256]{2,1,0:T(8,128)S(1)}, u32[]{:S(2)}, u32[]{:S(2)}) async-start(f32[64,32,256]{2,1,0:T(8,128)} %bitcast.26), calls=%async_computation | async-start | bytes 4194304 | tf_op jit(solution)/shard_map/all_to_all | solution.py:42
  51.0 0.0 reduce-scatter.2.cloned.1.call-start
  51.1 0.0 copy-done
  51.1 0.1 fusion.57
  51.2 0.4 compare_select_fusion
  51.6 49.1 %all-to-all-done = f32[64,32,256]{2,1,0:T(8,128)S(1)} async-done(((f32[64,32,256]{2,1,0:T(8,128)}), f32[64,32,256]{2,1,0:T(8,128)S(1)}, u32[]{:S(2)}, u32[]{:S(2)}) %all-to-all-start) | async-done | bytes 2097184 | tf_op jit(solution)/shard_map/all_to_all | solution.py:42
  100.7 3.1 fusion.52
  103.8 1.2 copy.9
  105.0 31.4 %gather_fusion = f32[8192,256]{1,0:T(8,128)} fusion(f32[2048,256]{1,0:T(8,128)S(1)} %bitcast.25, s32[8192]{0:T(1024)S(1)} %broadcast_clamp_fusion), kind=kCustom, calls=%fused_computation | custom fusion | bytes 16809984 | tf_op jit(solution)/shard_map/jit(_take)/gather | solution.py:59
  136.4 8.1 %select_select_fusion = f32[8192,256]{1,0:T(8,128)} fusion(f32[8192,256]{1,0:T(8,128)} %gather_fusion, pred[8192]{0:T(1024)(128)(4,1)S(1)} %get-tuple-element.3, pred[8192]{0:T(1024)(128)(4,1)S(1)} %get-tuple-element.2), kind=kLoop, calls=%fused_computation.26 | loop fusion | flops 4194304 | bytes 16793600 | tf_op jit(solution)/shard_map/jit(_where)/select_n | solution.py:61
  144.5 0.0 reduce-scatter.2.cloned.1.call-update
  144.5 0.0 all-reduce.2.cloned.1.call-start
  144.6 143.8 %reduce-scatter.2.cloned.1.call-done = f32[128,256]{1,0:T(8,128)} async-done(((f32[8192,256]{1,0:T(8,128)}), f32[128,256]{1,0:T(8,128)}) %reduce-scatter.2.cloned.1.call-update) | async-done | bytes 131088 | tf_op jit(solution)/shard_map/reduce_scatter | solution.py:60
  288.3 2.1 fusion.98
  290.4 0.0 all-reduce.2.cloned.1.call-update
  290.4 257.1 %all-reduce.2.cloned.1.call-done = f32[256,256]{1,0:T(8,128)} async-done(((f32[256,256]{1,0:T(8,128)}), f32[256,256]{1,0:T(8,128)}) %all-reduce.2.cloned.1.call-update) | async-done | bytes 262160 | tf_op jit(solution)/shard_map/psum | solution.py:66
  547.5 1.7 broadcast_multiply_fusion
  (9 shorter events, 0.1 us)
Async XLA Ops:
  9.9 41.2 %copy-start = (s32[1,8192]{1,0:T(1,128)S(1)}, s32[1,8192]{1,0:T(1,128)}, u32[]{:S(2)}) copy-start(s32[1,8192]{1,0:T(1,128)} %param.5) | copy-start | bytes 98308
  37.8 62.8 %all-to-all-start = ((f32[64,32,256]{2,1,0:T(8,128)}), f32[64,32,256]{2,1,0:T(8,128)S(1)}, u32[]{:S(2)}, u32[]{:S(2)}) async-start(f32[64,32,256]{2,1,0:T(8,128)} %bitcast.26), calls=%async_computation | async-start | bytes 4194304 | tf_op jit(solution)/shard_map/all_to_all | solution.py:42
  51.0 237.3 %reduce-scatter.2.cloned.1.call-start = ((), (), s32[]{:S(2)}) async-start(), calls=%async_computation.2 | async-start | bytes 8519680 | tf_op jit(solution)/shard_map/reduce_scatter | solution.py:60
  144.5 403.0 %all-reduce.2.cloned.1.call-start = ((), (), s32[]{:S(2)}) async-start(), calls=%async_computation.3 | async-start | bytes 524288 | tf_op jit(solution)/shard_map/psum | solution.py:66
Sparse Core Ops, SparseCore 0:
  144.6 143.6 reduce-scatter.1
  295.2 252.2 all-reduce.1
where the time goes:
time: 557 us; the launch traced here: 556 us
  waiting for transfers between devices  450 us (81%)
  matrix products  33.1 us (6%)
  local copies, waits for them, and re-layouts  32.6 us (6%)
  between operations  14.2 us (3%)
  starting transfers between devices  13.2 us (2%)
  other arithmetic  12.9 us (2%)
    psum x1, waiting for transfers between devices, shards(): gram = lax.psum(partial_gram, ('grp', 'dev')) / float(groups * samples)  257 us
    reduce_scatter x1, waiting for transfers between devices, shards(): lax.psum_scatter(jnp.where(mine[:, None], picked, 0.0), 'dev', scatter_di...  144 us
    all_to_all x1, waiting for transfers between devices, shards(): lax.all_to_all(local.reshape(devices, range_rows, width), 'dev', split_ax...  49.1 us
    gather x1, local copies, waits for them, and re-layouts, shards(): picked = jnp.take(owned_flat, place, axis=0)  31.4 us
    dot_general x1, matrix products, shards(): jnp.dot(walsh_table(rows_dev), signed, precision=lax.Precision.HIGHEST, p...  28 us
    all_to_all x1, starting transfers between devices, shards(): lax.all_to_all(local.reshape(devices, range_rows, width), 'dev', split_ax...  13.2 us
  transfers between devices with their start and end apart: 3, of which 3 were waited for; matrix products, arithmetic and copies ran while one was open for 0% of the time, Pallas kernels for 0%

commit v1 on v0

v1 whole, which is shorter than its diff:
```python
import functools
import math

import jax
import jax.numpy as jnp
from jax import lax
from jax.experimental import pallas as pl
from jax.experimental.pallas import tpu as pltpu
from jax.sharding import PartitionSpec as P

MESH = pl.DeviceIdType.MESH
F32 = jnp.float32
BF16 = jnp.bfloat16

PLANES = 8
PEERS = 8
CHUNKS = 8
IN_RANGE = 32
SLOTS = 4
BLOCKS = 64
HOLDERS = 32
LAG = 2


def butterfly(parts):
    span = 1
    while span < len(parts):
        out = list(parts)
        for a in range(len(parts)):
            if a & span == 0:
                out[a] = parts[a] + parts[a + span]
                out[a + span] = parts[a] - parts[a + span]
        parts = out
        span *= 2
    return parts


def split2(value):
    high = value.astype(BF16)
    return high, (value - high.astype(F32)).astype(BF16)


def dot(a, b):
    return jnp.dot(a, b, preferred_element_type=F32)


def dot_first(a, b):
    return lax.dot_general(a, b, (((0,), (0,)), ((), ())), preferred_element_type=F32)


def kernel(
    scale, gram_scale,
    design, bits, samples, sketch, gram,
    held, signs, table, arrived, partial, ring, code, owner, code_wide, pick,
    staged, slots, local, part_in, z_in,
    load_sem, y_send, y_recv, z_send, z_recv, d_send, d_recv,
    a_send, a_recv, b_send, b_recv, c_send, c_recv,
):
    g = lax.axis_index("grp")
    dev = lax.axis_index("dev")
    z = dev // PEERS
    p = dev % PEERS
    holder = g * PEERS + p

    def holder_id(k):
        other = holder ^ k
        return (other // PEERS, z * PEERS + other % PEERS)

    load = pltpu.make_async_copy(design, held, load_sem)
    load.start()

    barrier = pltpu.get_barrier_semaphore()
    for k in range(1, PLANES):
        pl.semaphore_signal(barrier, inc=1, device_id=(g, (z ^ k) * PEERS + p), device_id_type=MESH)

    def greet(k, carry):
        pl.semaphore_signal(barrier, inc=1, device_id=holder_id(k), device_id_type=MESH)
        return carry

    lax.fori_loop(1, HOLDERS, greet, 0)

    lane = lax.broadcasted_iota(jnp.int32, (128, 128), 1)
    row = lax.broadcasted_iota(jnp.int32, (128, 128), 0)
    ones = jnp.ones((128, 128), BF16)
    for i in range(16):
        sign = (2 * bits[pl.ds(i, 1), :] - 1).astype(F32)
        diagonal = jnp.where(lane == row, jnp.broadcast_to(sign, (128, 128)), 0.0)
        signs[pl.ds(i * 128, 128), :] = dot(diagonal.astype(BF16), ones)

    target = samples[...]
    owner[...] = (target >> 5) & 63
    along_z = (target >> 14) & z
    flip = (along_z ^ (along_z >> 1) ^ (along_z >> 2)) & 1
    code[...] = ((((target >> 11) & 7) << 5) | (target & 31) | (flip << 8) | 512).astype(F32)

    load.wait()

    def high_bits(i, carry):
        base = pl.multiple_of(i * IN_RANGE, IN_RANGE)
        for half in range(2):
            cols = pl.ds(half * 128, 128)
            parts = [
                held[pl.ds(k * 256 + base, IN_RANGE), cols] * signs[pl.ds(k * 256 + base, IN_RANGE), :]
                for k in range(8)
            ]
            for k, value in enumerate(butterfly(parts)):
                held[pl.ds(k * 256 + base, IN_RANGE), cols] = value
        return carry

    lax.fori_loop(0, 8, high_bits, 0)
    pl.semaphore_wait(barrier, PLANES - 1 + HOLDERS - 1)

    def y_copy(j, k):
        peer = p ^ k
        return pltpu.make_async_remote_copy(
            held.at[pl.ds(pl.multiple_of(j * 256 + peer * IN_RANGE, IN_RANGE), IN_RANGE)],
            arrived.at[j, pl.ds(pl.multiple_of(p * IN_RANGE, IN_RANGE), IN_RANGE)],
            y_send.at[j, k], y_recv.at[j, k],
            device_id=(g, z * PEERS + peer), device_id_type=MESH,
        )

    def y_landed(j, k):
        peer = p ^ k
        return pltpu.make_async_remote_copy(
            held.at[pl.ds(pl.multiple_of(j * 256 + p * IN_RANGE, IN_RANGE), IN_RANGE)],
            arrived.at[j, pl.ds(pl.multiple_of(peer * IN_RANGE, IN_RANGE), IN_RANGE)],
            y_send.at[j, k], y_recv.at[j, k],
            device_id=(g, z * PEERS + peer), device_id_type=MESH,
        )

    def low_bits(j, carry):
        base = pl.multiple_of(j * 256, 256)
        for half in range(2):
            cols = pl.ds(half * 128, 128)
            parts = [held[pl.ds(base + k * IN_RANGE, IN_RANGE), cols] for k in range(8)]
            for k, value in enumerate(butterfly(parts)):
                held[pl.ds(base + k * IN_RANGE, IN_RANGE), cols] = value
        for k in (4, 5, 2, 3, 6, 7, 1):
            y_copy(j, k).start()
        mine = pl.multiple_of(p * IN_RANGE, IN_RANGE)
        arrived[j, pl.ds(mine, IN_RANGE), :] = held[pl.ds(base + mine, IN_RANGE), :]
        return carry

    lax.fori_loop(0, CHUNKS, low_bits, 0)

    before = (row < lane).astype(BF16)

    def build(j, carry):
        here = owner[...] == 8 * j + p
        rank = dot(here.astype(F32).astype(BF16), before)
        for i in range(SLOTS):
            chosen = jnp.where(here & (rank == float(i)), code[...], 0.0)
            column = jnp.sum(chosen, axis=1, keepdims=True)
            code_wide[pl.ds(i, BLOCKS, stride=SLOTS), :] = jnp.broadcast_to(column, (BLOCKS, 128))
        wide = code_wide[...].astype(jnp.int32)
        at = lax.broadcasted_iota(jnp.int32, (256, 128), 1) + 256
        for half in range(2):
            v = wide & (at + 128 * half)
            v = v ^ (v >> 8)
            v = v ^ (v >> 4)
            v = v ^ (v >> 2)
            v = v ^ (v >> 1)
            value = jnp.where(wide >= 512, 1 - 2 * (v & 1), 0).astype(F32)
            table[j, :, pl.ds(half * 128, 128)] = value.astype(BF16)
        return carry

    lax.fori_loop(0, CHUNKS, build, 0)

    own = jnp.broadcast_to((samples[pl.ds(dev, 1), :] >> 5) & 63, (128, 128)).astype(F32)
    same = jnp.where((own == own.T) & (row < lane), 1.0, 0.0)
    rank = jnp.broadcast_to(jnp.sum(same, axis=0, keepdims=True), (128, 128))
    own = own.astype(jnp.int32)
    place = ((own & 7) * 32 + (own >> 3) * 4).astype(F32) + rank
    place = place.T
    for half in range(2):
        at = (lane + 128 * half).astype(F32)
        pick[:, pl.ds(half * 128, 128)] = jnp.where(place == at, 1.0, 0.0).astype(BF16)

    local[...] = jnp.zeros_like(local)

    def block(index):
        return pl.ds(pl.multiple_of(index * 32, 32), 32)

    def hop(j, way, step, source):
        step_z = 1 if way == 0 else PLANES - 1
        return pltpu.make_async_remote_copy(
            source, ring.at[j, way, step], z_send.at[j, way, step], z_recv.at[j, way, step],
            device_id=(g, (z + step_z) % PLANES * PEERS + p), device_id_type=MESH,
        )

    def reach(j, way):
        return 3 + (j + way + 1) % 2

    def dest(j, way, step):
        far = reach(j, way) - step
        return (z + far) % PLANES if way == 0 else (z + PLANES - far) % PLANES

    def produce(j):
        for k in range(1, PEERS):
            y_landed(j, k).wait_recv()
        high, low = split2(arrived[j])
        partial[j] = dot(table[j], high) + dot(table[j], low)
        for way in range(2):
            hop(j, way, 0, partial.at[j, block(dest(j, way, 0))]).start()

    def deliver(m, k):
        peer = p ^ k
        return pltpu.make_async_remote_copy(
            staged.at[m, peer], slots.at[pl.ds(pl.multiple_of(p * 32 + m * 8, 8), 8)],
            d_send.at[m, k], d_recv.at[m, k],
            device_id=(g, z * PEERS + peer), device_id_type=MESH,
        )

    def delivered(m, k):
        peer = p ^ k
        return pltpu.make_async_remote_copy(
            staged.at[m, p], slots.at[pl.ds(pl.multiple_of(peer * 32 + m * 8, 8), 8)],
            d_send.at[m, k], d_recv.at[m, k],
            device_id=(g, z * PEERS + peer), device_id_type=MESH,
        )

    def forward(j, step):
        for way in range(2):
            def take(way=way):
                hop(j, way, step - 1, partial.at[j, block(0)]).wait_recv()

            def send(way=way):
                ring[j, way, step - 1] += partial[j, block(dest(j, way, step)), :]
                hop(j, way, step, ring.at[j, way, step - 1]).start()

            if step <= 2:
                take()
                send()
            elif step == 3:
                take()
                pl.when(reach(j, way) == 4)(send)
            else:
                pl.when(reach(j, way) == 4)(take)

    def finish(j):
        done = partial[j, block(z), :]
        for way in range(2):
            done = done + ring[j, way, reach(j, way) - 1]
        m = j // 2
        for odd in range(2):

            @pl.when(j % 2 == odd)
            def _(odd=odd):
                for k in range(PEERS):
                    staged[m, k, pl.ds(odd * SLOTS, SLOTS), :] = done[k * SLOTS : (k + 1) * SLOTS, :]

        high, low = split2(done)
        local[...] += dot_first(high, high) + dot_first(high, low) + dot_first(low, high)

        @pl.when(j % 2 == 1)
        def _():
            for k in (4, 5, 2, 3, 6, 7, 1):
                deliver(m, k).start()
            slots[pl.ds(pl.multiple_of(p * 32 + m * 8, 8), 8), :] = staged[m, p]

    def turn(t, carry):
        @pl.when(t < CHUNKS)
        def _():
            produce(t)

        for step in range(1, 5):
            j = t - LAG * step

            @pl.when((j >= 0) & (j < CHUNKS))
            def _(j=j, step=step):
                forward(j, step)
                if step == 4:
                    finish(j)

        return carry

    lax.fori_loop(0, CHUNKS + 4 * LAG, turn, 0)

    def rows(index):
        return pl.ds(pl.multiple_of(index * 8, 8), 8)

    def copy_a(k):
        return pltpu.make_async_remote_copy(
            local.at[rows(holder ^ k)], part_in.at[holder], a_send.at[k], a_recv.at[k],
            device_id=holder_id(k), device_id_type=MESH,
        )

    def landed_a(k):
        return pltpu.make_async_remote_copy(
            local.at[rows(holder)], part_in.at[holder ^ k], a_send.at[k], a_recv.at[k],
            device_id=holder_id(k), device_id_type=MESH,
        )

    def copy_b(k):
        return pltpu.make_async_remote_copy(
            z_in.at[z], z_in.at[z], b_send.at[k], b_recv.at[k],
            device_id=(g, (z ^ k) * PEERS + p), device_id_type=MESH,
        )

    def landed_b(k):
        return pltpu.make_async_remote_copy(
            z_in.at[z], z_in.at[z ^ k], b_send.at[k], b_recv.at[k],
            device_id=(g, (z ^ k) * PEERS + p), device_id_type=MESH,
        )

    def copy_c(k):
        return pltpu.make_async_remote_copy(
            gram.at[rows(holder)], gram.at[rows(holder)], c_send.at[k], c_recv.at[k],
            device_id=holder_id(k), device_id_type=MESH,
        )

    def landed_c(k):
        return pltpu.make_async_remote_copy(
            gram.at[rows(holder)], gram.at[rows(holder ^ k)], c_send.at[k], c_recv.at[k],
            device_id=holder_id(k), device_id_type=MESH,
        )

    def each(start, stop, act):
        def step(k, carry):
            act(k)
            return carry

        lax.fori_loop(start, stop, step, 0)

    each(1, HOLDERS, lambda k: copy_a(HOLDERS - k).start())

    part_in[holder] = local[rows(holder), :]
    for m in range(CHUNKS // 2):
        for k in range(1, PEERS):
            delivered(m, k).wait_recv()
    value = slots[...]
    first, rest = split2(value)
    second, third = split2(value - first.astype(F32))
    sketch[...] = (dot(pick[...], first) + dot(pick[...], second) + dot(pick[...], third)) * scale

    each(1, HOLDERS, lambda k: landed_a(k).wait_recv())
    z_in[z] = jnp.sum(part_in[...], axis=0)
    each(1, PLANES, lambda k: copy_b(PLANES - k).start())
    each(1, PLANES, lambda k: landed_b(k).wait_recv())
    gram[rows(holder), :] = jnp.sum(z_in[...], axis=0) * gram_scale
    each(1, HOLDERS, lambda k: copy_c(HOLDERS - k).start())
    each(1, HOLDERS, lambda k: landed_c(k).wait_recv())

    def y_sent(j, carry):
        for k in range(1, PEERS):
            y_copy(j, k).wait_send()
        for way in range(2):
            for step in range(3):
                hop(j, way, step, ring.at[j, way, step]).wait_send()

            @pl.when(reach(j, way) == 4)
            def _(way=way):
                hop(j, way, 3, ring.at[j, way, 2]).wait_send()
        return carry

    lax.fori_loop(0, CHUNKS, y_sent, 0)
    for m in range(CHUNKS // 2):
        for k in range(1, PEERS):
            deliver(m, k).wait_send()
    each(1, HOLDERS, lambda k: copy_a(k).wait_send())
    each(1, PLANES, lambda k: copy_b(k).wait_send())
    each(1, HOLDERS, lambda k: copy_c(k).wait_send())


def shards(design, sign_bits, sample_rows):
    rows, width = design.shape
    slab = rows * lax.axis_size("dev")
    total = lax.axis_size("grp") * sample_rows.shape[1]
    vmem = pl.BlockSpec(memory_space=pltpu.VMEM)
    dma = pltpu.SemaphoreType.DMA
    return pl.pallas_call(
        functools.partial(kernel, 1.0 / math.sqrt(slab), 1.0 / (slab * total)),
        out_shape=(
            jax.ShapeDtypeStruct((128, width), F32),
            jax.ShapeDtypeStruct((width, width), F32),
        ),
        in_specs=[pl.BlockSpec(memory_space=pl.ANY), vmem, vmem],
        out_specs=(vmem, vmem),
        scratch_shapes=[
            pltpu.VMEM((2048, 256), F32),
            pltpu.VMEM((2048, 128), F32),
            pltpu.VMEM((CHUNKS, 256, 256), BF16),
            pltpu.VMEM((CHUNKS, 256, 256), F32),
            pltpu.VMEM((CHUNKS, 256, 256), F32),
            pltpu.VMEM((CHUNKS, 2, 4, 32, 256), F32),
            pltpu.VMEM((BLOCKS, 128), F32),
            pltpu.VMEM((BLOCKS, 128), jnp.int32),
            pltpu.VMEM((256, 128), F32),
            pltpu.VMEM((128, 256), BF16),
            pltpu.VMEM((CHUNKS // 2, PEERS, 8, 256), F32),
            pltpu.VMEM((256, 256), F32),
            pltpu.VMEM((256, 256), F32),
            pltpu.VMEM((HOLDERS, 8, 256), F32),
            pltpu.VMEM((PLANES, 8, 256), F32),
            dma,
            dma((CHUNKS, PEERS)), dma((CHUNKS, PEERS)),
            dma((CHUNKS, 2, 4)), dma((CHUNKS, 2, 4)),
            dma((CHUNKS // 2, PEERS)), dma((CHUNKS // 2, PEERS)),
            dma((HOLDERS,)), dma((HOLDERS,)),
            dma((PLANES,)), dma((PLANES,)),
            dma((HOLDERS,)), dma((HOLDERS,)),
        ],
        compiler_params=pltpu.CompilerParams(
            collective_id=0, has_side_effects=True, vmem_limit_bytes=32 << 20
        ),
        cost_estimate=pl.CostEstimate(flops=2 * 10**9, bytes_accessed=4 << 20, transcendentals=0),
    )(design, sign_bits.reshape(16, 128), sample_rows.reshape(BLOCKS, 128))


def solution(mesh):
    return jax.shard_map(
        shards,
        mesh=mesh,
        in_specs=(P(("grp", "dev"), None), P(("grp", "dev")), P("grp", None)),
        out_specs=(P(("grp", "dev"), None), P()),
        check_vma=False,
    )
```

time: 557 us -> 76.1 us (0.14)
  waiting for transfers between devices: 450 us -> 0 us
  Pallas kernels: 0 us -> 70.8 us
  matrix products: 33.1 us -> 0 us
  local copies, waits for them, and re-layouts: 32.6 us -> 4.4 us
  between operations: 14.2 us -> 0.65 us
  starting transfers between devices: 13.2 us -> 0 us
  other arithmetic: 12.9 us -> 0 us
    psum x1 -> x0, waiting for transfers between devices: 257 us -> none  [shards(): gram = lax.psum(partial_gram, ('grp', 'dev')) / float(groups * samples)]
    reduce_scatter x1 -> x0, waiting for transfers between devices: 144 us -> none  [shards(): lax.psum_scatter(jnp.where(mine[:, None], picked, 0.0), 'dev', scatter_di...]
    pallas_call x0 -> x1, Pallas kernels: none -> 70.8 us  [shards(): pl.pallas_call(functools.partial(kernel, 1.0 / math.sqrt(slab), 1.0 / (sl...]
    all_to_all x1 -> x0, waiting for transfers between devices: 49.1 us -> none  [shards(): lax.all_to_all(local.reshape(devices, range_rows, width), 'dev', split_ax...]
    dot_general x3 -> x0, matrix products: 33.1 us -> none  [the longest x1 28 us: shards(): jnp.dot(walsh_table(rows_dev), signed, precision=lax.Precision.HIGHEST, p...]
    gather x1 -> x0, local copies, waits for them, and re-layouts: 31.4 us -> none  [shards(): picked = jnp.take(owned_flat, place, axis=0)]
    all_to_all x1 -> x0, starting transfers between devices: 13.2 us -> none  [shards(): lax.all_to_all(local.reshape(devices, range_rows, width), 'dev', split_ax...]
    select_n x2 -> x0, other arithmetic: 8.47 us -> none  [the longest x1 8.11 us: shards(): jnp.where(mine[:, None], picked, 0.0)]
  transfers between devices with their start and end apart: 3 -> 0, of which waited for: 3 -> 0; matrix products, arithmetic and copies ran while one was open for 0% -> 0% of each run, Pallas kernels for 0% -> 0%
where the time goes in v1:
time: 76.1 us; the launch traced here: 75.9 us
  Pallas kernels  70.8 us (93%)
  local copies, waits for them, and re-layouts  4.4 us (6%)
    pallas_call x1, Pallas kernels, shards(): pl.pallas_call(functools.partial(kernel, 1.0 / math.sqrt(slab), 1.0 / (sl...  70.8 us
    unnamed x8, local copies, waits for them, and re-layouts  4.4 us

profile of v1, /device:TPU:1, one launch (start us, length us, event | category | flops | bytes accessed | tf_op | source)
XLA Modules:
  0.0 75.9 jit_solution(14491380925908113211)
XLA Ops:
  0.6 0.0 copy-start
  0.6 1.6 %copy-done = f32[2048,256]{1,0:T(8,128)S(1)} copy-done((f32[2048,256]{1,0:T(8,128)S(1)}, f32[2048,256]{1,0:T(8,128)}, u32[]{:S(2)}) %copy-start) | copy-done | bytes 2097176
  2.2 0.0 copy-start.1
  2.2 0.8 copy-done.1
  3.0 0.0 copy-start.2
  3.0 0.7 copy-done.2
  3.7 70.8 %shard_map.50 = (f32[128,256]{1,0:T(8,128)S(1)}, f32[256,256]{1,0:T(8,128)S(1)}) custom-call(f32[2048,256]{1,0:T(8,128)S(1)} %copy-done, s32[16,128]{1,0:T(8,128)S(1)} %bitcast.3, s32[64,128]{1,0:T(8,128)S(1)} %bitcast.2), custom_call_target="tpu_custom_call" | custom-call | flops 2000000000 | bytes 4194304 | tf_op jit(solution)/shard_map/pallas_call | solution.py:371
  74.5 0.7 copy.7
  75.2 0.7 copy.8
Async XLA Ops:
  0.6 1.6 %copy-start = (f32[2048,256]{1,0:T(8,128)S(1)}, f32[2048,256]{1,0:T(8,128)}, u32[]{:S(2)}) copy-start(f32[2048,256]{1,0:T(8,128)} %design.1) | copy-start | bytes 6291460
  2.2 0.8 copy-start.1
  3.0 0.7 copy-start.2

commit v2 on v1

--- a/solution.py
+++ b/solution.py
@@ -12,6 +12,7 @@
 F32 = jnp.float32
 BF16 = jnp.bfloat16
 
+GROUPS = 4
 PLANES = 8
 PEERS = 8
 CHUNKS = 8
@@ -19,6 +20,7 @@
 SLOTS = 4
 BLOCKS = 64
 HOLDERS = 32
+FAR_FIRST = tuple(k ^ 20 for k in range(HOLDERS) if k != 20)
 LAG = 2
 
 
@@ -50,10 +52,10 @@
 
 def kernel(
     scale, gram_scale,
-    design, bits, samples, sketch, gram,
+    design, small, sketch, gram,
     held, signs, table, arrived, partial, ring, code, owner, code_wide, pick,
     staged, slots, local, part_in, z_in,
-    load_sem, y_send, y_recv, z_send, z_recv, d_send, d_recv,
+    load_sem, ready, y_send, y_recv, z_send, z_recv, d_send, d_recv,
     a_send, a_recv, b_send, b_recv, c_send, c_recv,
 ):
     g = lax.axis_index("grp")
@@ -66,54 +68,53 @@
         other = holder ^ k
         return (other // PEERS, z * PEERS + other % PEERS)
 
-    load = pltpu.make_async_copy(design, held, load_sem)
-    load.start()
+    loads = [
+        pltpu.make_async_copy(
+            design.at[:, pl.ds(i * 64, 64)], held.at[:, pl.ds(i * 64, 64)], load_sem.at[i]
+        )
+        for i in range(4)
+    ]
+    for load in loads:
+        load.start()
 
     barrier = pltpu.get_barrier_semaphore()
     for k in range(1, PLANES):
+        pl.semaphore_signal(barrier, inc=1, device_id=(g, z * PEERS + (p ^ k)), device_id_type=MESH)
         pl.semaphore_signal(barrier, inc=1, device_id=(g, (z ^ k) * PEERS + p), device_id_type=MESH)
-
-    def greet(k, carry):
-        pl.semaphore_signal(barrier, inc=1, device_id=holder_id(k), device_id_type=MESH)
-        return carry
-
-    lax.fori_loop(1, HOLDERS, greet, 0)
+    for k in range(1, GROUPS):
+        pl.semaphore_signal(barrier, inc=1, device_id=(g ^ k, dev), device_id_type=MESH)
 
     lane = lax.broadcasted_iota(jnp.int32, (128, 128), 1)
     row = lax.broadcasted_iota(jnp.int32, (128, 128), 0)
     ones = jnp.ones((128, 128), BF16)
     for i in range(16):
-        sign = (2 * bits[pl.ds(i, 1), :] - 1).astype(F32)
+        sign = (2 * small[pl.ds(BLOCKS + i, 1), :] - 1).astype(F32)
         diagonal = jnp.where(lane == row, jnp.broadcast_to(sign, (128, 128)), 0.0)
         signs[pl.ds(i * 128, 128), :] = dot(diagonal.astype(BF16), ones)
 
-    target = samples[...]
+    target = small[pl.ds(0, BLOCKS), :]
     owner[...] = (target >> 5) & 63
     along_z = (target >> 14) & z
     flip = (along_z ^ (along_z >> 1) ^ (along_z >> 2)) & 1
     code[...] = ((((target >> 11) & 7) << 5) | (target & 31) | (flip << 8) | 512).astype(F32)
 
-    load.wait()
-
-    def high_bits(i, carry):
-        base = pl.multiple_of(i * IN_RANGE, IN_RANGE)
+    for i in range(8):
+        if i % 2 == 0:
+            loads[i // 2].wait()
+        rows_in = pl.ds(i * IN_RANGE, IN_RANGE)
         for half in range(2):
             cols = pl.ds(half * 128, 128)
             parts = [
-                held[pl.ds(k * 256 + base, IN_RANGE), cols] * signs[pl.ds(k * 256 + base, IN_RANGE), :]
+                held[k, rows_in, cols] * signs[pl.ds(k * 256 + i * IN_RANGE, IN_RANGE), :]
                 for k in range(8)
             ]
             for k, value in enumerate(butterfly(parts)):
-                held[pl.ds(k * 256 + base, IN_RANGE), cols] = value
-        return carry
-
-    lax.fori_loop(0, 8, high_bits, 0)
-    pl.semaphore_wait(barrier, PLANES - 1 + HOLDERS - 1)
+                held[k, rows_in, cols] = value
 
     def y_copy(j, k):
         peer = p ^ k
         return pltpu.make_async_remote_copy(
-            held.at[pl.ds(pl.multiple_of(j * 256 + peer * IN_RANGE, IN_RANGE), IN_RANGE)],
+            held.at[j, pl.ds(pl.multiple_of(peer * IN_RANGE, IN_RANGE), IN_RANGE)],
             arrived.at[j, pl.ds(pl.multiple_of(p * IN_RANGE, IN_RANGE), IN_RANGE)],
             y_send.at[j, k], y_recv.at[j, k],
             device_id=(g, z * PEERS + peer), device_id_type=MESH,
@@ -122,26 +123,33 @@
     def y_landed(j, k):
         peer = p ^ k
         return pltpu.make_async_remote_copy(
-            held.at[pl.ds(pl.multiple_of(j * 256 + p * IN_RANGE, IN_RANGE), IN_RANGE)],
+            held.at[j, pl.ds(pl.multiple_of(p * IN_RANGE, IN_RANGE), IN_RANGE)],
             arrived.at[j, pl.ds(pl.multiple_of(peer * IN_RANGE, IN_RANGE), IN_RANGE)],
             y_send.at[j, k], y_recv.at[j, k],
             device_id=(g, z * PEERS + peer), device_id_type=MESH,
         )
 
     def low_bits(j, carry):
-        base = pl.multiple_of(j * 256, 256)
         for half in range(2):
             cols = pl.ds(half * 128, 128)
-            parts = [held[pl.ds(base + k * IN_RANGE, IN_RANGE), cols] for k in range(8)]
+            parts = [held[j, pl.ds(k * IN_RANGE, IN_RANGE), cols] for k in range(8)]
             for k, value in enumerate(butterfly(parts)):
-                held[pl.ds(base + k * IN_RANGE, IN_RANGE), cols] = value
+                held[j, pl.ds(k * IN_RANGE, IN_RANGE), cols] = value
+
+        @pl.when(j == 0)
+        def _():
+            pl.semaphore_wait(barrier, PEERS - 1 + PLANES - 1 + GROUPS - 1)
+
         for k in (4, 5, 2, 3, 6, 7, 1):
             y_copy(j, k).start()
         mine = pl.multiple_of(p * IN_RANGE, IN_RANGE)
-        arrived[j, pl.ds(mine, IN_RANGE), :] = held[pl.ds(base + mine, IN_RANGE), :]
+        arrived[j, pl.ds(mine, IN_RANGE), :] = held[j, pl.ds(mine, IN_RANGE), :]
         return carry
 
     lax.fori_loop(0, CHUNKS, low_bits, 0)
+
+    for k in range(1, GROUPS):
+        pl.semaphore_signal(ready, inc=1, device_id=(g ^ k, dev), device_id_type=MESH)
 
     before = (row < lane).astype(BF16)
 
@@ -166,7 +174,7 @@
 
     lax.fori_loop(0, CHUNKS, build, 0)
 
-    own = jnp.broadcast_to((samples[pl.ds(dev, 1), :] >> 5) & 63, (128, 128)).astype(F32)
+    own = jnp.broadcast_to((small[pl.ds(dev, 1), :] >> 5) & 63, (128, 128)).astype(F32)
     same = jnp.where((own == own.T) & (row < lane), 1.0, 0.0)
     rank = jnp.broadcast_to(jnp.sum(same, axis=0, keepdims=True), (128, 128))
     own = own.astype(jnp.int32)
@@ -219,6 +227,11 @@
             device_id=(g, z * PEERS + peer), device_id_type=MESH,
         )
 
+    def send_pair(m):
+        for k in (4, 5, 2, 3, 6, 7, 1):
+            deliver(m, k).start()
+        slots[pl.ds(pl.multiple_of(p * 32 + m * 8, 8), 8), :] = staged[m, p]
+
     def forward(j, step):
         for way in range(2):
             def take(way=way):
@@ -252,11 +265,9 @@
         high, low = split2(done)
         local[...] += dot_first(high, high) + dot_first(high, low) + dot_first(low, high)
 
-        @pl.when(j % 2 == 1)
+        @pl.when((j % 2 == 1) & (j < CHUNKS - 1))
         def _():
-            for k in (4, 5, 2, 3, 6, 7, 1):
-                deliver(m, k).start()
-            slots[pl.ds(pl.multiple_of(p * 32 + m * 8, 8), 8), :] = staged[m, p]
+            send_pair(m)
 
     def turn(t, carry):
         @pl.when(t < CHUNKS)
@@ -281,67 +292,33 @@
 
     def copy_a(k):
         return pltpu.make_async_remote_copy(
-            local.at[rows(holder ^ k)], part_in.at[holder], a_send.at[k], a_recv.at[k],
+            local.at[rows(holder ^ k)], part_in.at[rows(holder)], a_send, a_recv,
             device_id=holder_id(k), device_id_type=MESH,
         )
 
-    def landed_a(k):
-        return pltpu.make_async_remote_copy(
-            local.at[rows(holder)], part_in.at[holder ^ k], a_send.at[k], a_recv.at[k],
+    def copy_b(k):
+        return pltpu.make_async_remote_copy(
+            z_in.at[rows(z)], z_in.at[rows(z)], b_send, b_recv,
+            device_id=(g, (z ^ k) * PEERS + p), device_id_type=MESH,
+        )
+
+    def copy_c(k):
+        return pltpu.make_async_remote_copy(
+            gram.at[rows(holder)], gram.at[rows(holder)], c_send, c_recv,
             device_id=holder_id(k), device_id_type=MESH,
         )
 
-    def copy_b(k):
-        return pltpu.make_async_remote_copy(
-            z_in.at[z], z_in.at[z], b_send.at[k], b_recv.at[k],
-            device_id=(g, (z ^ k) * PEERS + p), device_id_type=MESH,
-        )
-
-    def landed_b(k):
-        return pltpu.make_async_remote_copy(
-            z_in.at[z], z_in.at[z ^ k], b_send.at[k], b_recv.at[k],
-            device_id=(g, (z ^ k) * PEERS + p), device_id_type=MESH,
-        )
-
-    def copy_c(k):
-        return pltpu.make_async_remote_copy(
-            gram.at[rows(holder)], gram.at[rows(holder)], c_send.at[k], c_recv.at[k],
-            device_id=holder_id(k), device_id_type=MESH,
-        )
-
-    def landed_c(k):
-        return pltpu.make_async_remote_copy(
-            gram.at[rows(holder)], gram.at[rows(holder ^ k)], c_send.at[k], c_recv.at[k],
-            device_id=holder_id(k), device_id_type=MESH,
-        )
-
-    def each(start, stop, act):
-        def step(k, carry):
-            act(k)
-            return carry
-
-        lax.fori_loop(start, stop, step, 0)
-
-    each(1, HOLDERS, lambda k: copy_a(HOLDERS - k).start())
-
-    part_in[holder] = local[rows(holder), :]
-    for m in range(CHUNKS // 2):
-        for k in range(1, PEERS):
-            delivered(m, k).wait_recv()
-    value = slots[...]
-    first, rest = split2(value)
-    second, third = split2(value - first.astype(F32))
-    sketch[...] = (dot(pick[...], first) + dot(pick[...], second) + dot(pick[...], third)) * scale
-
-    each(1, HOLDERS, lambda k: landed_a(k).wait_recv())
-    z_in[z] = jnp.sum(part_in[...], axis=0)
-    each(1, PLANES, lambda k: copy_b(PLANES - k).start())
-    each(1, PLANES, lambda k: landed_b(k).wait_recv())
-    gram[rows(holder), :] = jnp.sum(z_in[...], axis=0) * gram_scale
-    each(1, HOLDERS, lambda k: copy_c(HOLDERS - k).start())
-    each(1, HOLDERS, lambda k: landed_c(k).wait_recv())
-
-    def y_sent(j, carry):
+    def wait_all(ref, count, sem):
+        whole = ref.at[pl.ds(0, count * 8)]
+        pltpu.make_async_copy(whole, whole, sem).wait()
+
+    pl.semaphore_wait(ready, GROUPS - 1)
+    for k in FAR_FIRST:
+        copy_a(k).start()
+    part_in[rows(holder), :] = local[rows(holder), :]
+    send_pair(CHUNKS // 2 - 1)
+
+    def gone(j, carry):
         for k in range(1, PEERS):
             y_copy(j, k).wait_send()
         for way in range(2):
@@ -353,13 +330,29 @@
                 hop(j, way, 3, ring.at[j, way, 2]).wait_send()
         return carry
 
-    lax.fori_loop(0, CHUNKS, y_sent, 0)
+    lax.fori_loop(0, CHUNKS, gone, 0)
+
     for m in range(CHUNKS // 2):
         for k in range(1, PEERS):
+            delivered(m, k).wait_recv()
             deliver(m, k).wait_send()
-    each(1, HOLDERS, lambda k: copy_a(k).wait_send())
-    each(1, PLANES, lambda k: copy_b(k).wait_send())
-    each(1, HOLDERS, lambda k: copy_c(k).wait_send())
+    value = slots[...]
+    first, rest = split2(value)
+    second, third = split2(value - first.astype(F32))
+    sketch[...] = (dot(pick[...], first) + dot(pick[...], second) + dot(pick[...], third)) * scale
+
+    wait_all(part_in, HOLDERS - 1, a_recv)
+    z_in[rows(z), :] = jnp.sum(part_in[...].reshape(HOLDERS, 8, 256), axis=0)
+    for k in (4, 3, 5, 2, 6, 1, 7):
+        copy_b(k).start()
+    wait_all(part_in, HOLDERS - 1, a_send)
+    wait_all(z_in, PLANES - 1, b_recv)
+    gram[rows(holder), :] = jnp.sum(z_in[...].reshape(PLANES, 8, 256), axis=0) * gram_scale
+    for k in FAR_FIRST:
+        copy_c(k).start()
+    wait_all(z_in, PLANES - 1, b_send)
+    wait_all(gram, HOLDERS - 1, c_recv)
+    wait_all(gram, HOLDERS - 1, c_send)
 
 
 def shards(design, sign_bits, sample_rows):
@@ -367,6 +360,7 @@
     slab = rows * lax.axis_size("dev")
     total = lax.axis_size("grp") * sample_rows.shape[1]
     vmem = pl.BlockSpec(memory_space=pltpu.VMEM)
+    small = jnp.concatenate([sample_rows.reshape(BLOCKS, 128), sign_bits.reshape(16, 128)])
     dma = pltpu.SemaphoreType.DMA
     return pl.pallas_call(
         functools.partial(kernel, 1.0 / math.sqrt(slab), 1.0 / (slab * total)),
@@ -374,10 +368,10 @@
             jax.ShapeDtypeStruct((128, width), F32),
             jax.ShapeDtypeStruct((width, width), F32),
         ),
-        in_specs=[pl.BlockSpec(memory_space=pl.ANY), vmem, vmem],
+        in_specs=[pl.BlockSpec(memory_space=pltpu.HBM), vmem],
         out_specs=(vmem, vmem),
         scratch_shapes=[
-            pltpu.VMEM((2048, 256), F32),
+            pltpu.VMEM((CHUNKS, 256, 256), F32),
             pltpu.VMEM((2048, 128), F32),
             pltpu.VMEM((CHUNKS, 256, 256), BF16),
             pltpu.VMEM((CHUNKS, 256, 256), F32),
@@ -390,21 +384,20 @@
             pltpu.VMEM((CHUNKS // 2, PEERS, 8, 256), F32),
             pltpu.VMEM((256, 256), F32),
             pltpu.VMEM((256, 256), F32),
-            pltpu.VMEM((HOLDERS, 8, 256), F32),
-            pltpu.VMEM((PLANES, 8, 256), F32),
-            dma,
+            pltpu.VMEM((HOLDERS * 8, 256), F32),
+            pltpu.VMEM((PLANES * 8, 256), F32),
+            dma((4,)),
+            pltpu.SemaphoreType.REGULAR,
             dma((CHUNKS, PEERS)), dma((CHUNKS, PEERS)),
             dma((CHUNKS, 2, 4)), dma((CHUNKS, 2, 4)),
             dma((CHUNKS // 2, PEERS)), dma((CHUNKS // 2, PEERS)),
-            dma((HOLDERS,)), dma((HOLDERS,)),
-            dma((PLANES,)), dma((PLANES,)),
-            dma((HOLDERS,)), dma((HOLDERS,)),
+            dma, dma, dma, dma, dma, dma,
         ],
         compiler_params=pltpu.CompilerParams(
-            collective_id=0, has_side_effects=True, vmem_limit_bytes=32 << 20
+            collective_id=0, has_side_effects=True, vmem_limit_bytes=52 << 20
         ),
         cost_estimate=pl.CostEstimate(flops=2 * 10**9, bytes_accessed=4 << 20, transcendentals=0),
-    )(design, sign_bits.reshape(16, 128), sample_rows.reshape(BLOCKS, 128))
+    )(design.reshape(CHUNKS, 256, width), small)
 
 
 def solution(mesh):

time: 76.1 us -> 71.1 us (0.934)
  local copies, waits for them, and re-layouts: 4.4 us -> 1.36 us
  Pallas kernels: 70.8 us -> 68.2 us
  other arithmetic: 0 us -> 0.78 us
    unnamed x8 -> x2, local copies, waits for them, and re-layouts: 4.4 us -> 1.36 us
    pallas_call x1, Pallas kernels: 70.8 us -> 68.2 us  [shards(): pl.pallas_call(functools.partial(kernel, 1.0 / math.sqrt(slab), 1.0 / (sl...]
    concatenate x0 -> x1, other arithmetic: none -> 0.78 us  [shards(): jnp.concatenate([sample_rows.reshape(BLOCKS, 128), sign_bits.reshape(16,...]
where the time goes in v2:
time: 71.1 us; the launch traced here: 70.9 us
  Pallas kernels  68.2 us (96%)
  local copies, waits for them, and re-layouts  1.36 us (2%)
  other arithmetic  0.78 us (1%)
    pallas_call x1, Pallas kernels, shards(): pl.pallas_call(functools.partial(kernel, 1.0 / math.sqrt(slab), 1.0 / (sl...  68.2 us

profile of v2, /device:TPU:1, one launch (start us, length us, event | category | flops | bytes accessed | tf_op | source)
XLA Modules:
  0.0 70.9 jit_solution(10710251219783849892)
XLA Ops:
  0.6 0.8 %pad_add_fusion.small = s32[80,128]{1,0:T(8,128)S(1)} fusion(s32[16,128]{1,0:T(8,128)} %bitcast.4, s32[64,128]{1,0:T(8,128)} %bitcast.3), kind=kLoop, calls=%fused_computation | loop fusion | flops 10240 | bytes 81920 | tf_op jit(solution)/shard_map/concatenate | solution.py:363
  1.4 68.2 %shard_map.50 = (f32[128,256]{1,0:T(8,128)S(1)}, f32[256,256]{1,0:T(8,128)S(1)}) custom-call(f32[8,256,256]{2,1,0:T(8,128)} %bitcast.5, s32[80,128]{1,0:T(8,128)S(1)} %pad_add_fusion.small), custom_call_target="tpu_custom_call" | custom-call | flops 2000000000 | bytes 4194304 | tf_op jit(solution)/shard_map/pallas_call | solution.py:365
  69.6 0.7 copy.7
  70.2 0.7 copy.8

commit v3 on v2

--- a/solution.py
+++ b/solution.py
@@ -116,18 +116,12 @@
         return pltpu.make_async_remote_copy(
             held.at[j, pl.ds(pl.multiple_of(peer * IN_RANGE, IN_RANGE), IN_RANGE)],
             arrived.at[j, pl.ds(pl.multiple_of(p * IN_RANGE, IN_RANGE), IN_RANGE)],
-            y_send.at[j, k], y_recv.at[j, k],
+            y_send, y_recv.at[j],
             device_id=(g, z * PEERS + peer), device_id_type=MESH,
         )
 
-    def y_landed(j, k):
-        peer = p ^ k
-        return pltpu.make_async_remote_copy(
-            held.at[j, pl.ds(pl.multiple_of(p * IN_RANGE, IN_RANGE), IN_RANGE)],
-            arrived.at[j, pl.ds(pl.multiple_of(peer * IN_RANGE, IN_RANGE), IN_RANGE)],
-            y_send.at[j, k], y_recv.at[j, k],
-            device_id=(g, z * PEERS + peer), device_id_type=MESH,
-        )
+    def wait_bytes(ref, sem):
+        pltpu.make_async_copy(ref, ref, sem).wait()
 
     def low_bits(j, carry):
         for half in range(2):
@@ -192,7 +186,7 @@
     def hop(j, way, step, source):
         step_z = 1 if way == 0 else PLANES - 1
         return pltpu.make_async_remote_copy(
-            source, ring.at[j, way, step], z_send.at[j, way, step], z_recv.at[j, way, step],
+            source, ring.at[j, step, way], z_send, z_recv.at[j, step],
             device_id=(g, (z + step_z) % PLANES * PEERS + p), device_id_type=MESH,
         )
 
@@ -204,8 +198,7 @@
         return (z + far) % PLANES if way == 0 else (z + PLANES - far) % PLANES
 
     def produce(j):
-        for k in range(1, PEERS):
-            y_landed(j, k).wait_recv()
+        wait_bytes(arrived.at[j, pl.ds(0, (PEERS - 1) * IN_RANGE)], y_recv.at[j])
         high, low = split2(arrived[j])
         partial[j] = dot(table[j], high) + dot(table[j], low)
         for way in range(2):
@@ -215,15 +208,7 @@
         peer = p ^ k
         return pltpu.make_async_remote_copy(
             staged.at[m, peer], slots.at[pl.ds(pl.multiple_of(p * 32 + m * 8, 8), 8)],
-            d_send.at[m, k], d_recv.at[m, k],
-            device_id=(g, z * PEERS + peer), device_id_type=MESH,
-        )
-
-    def delivered(m, k):
-        peer = p ^ k
-        return pltpu.make_async_remote_copy(
-            staged.at[m, p], slots.at[pl.ds(pl.multiple_of(peer * 32 + m * 8, 8), 8)],
-            d_send.at[m, k], d_recv.at[m, k],
+            d_send, d_recv,
             device_id=(g, z * PEERS + peer), device_id_type=MESH,
         )
 
@@ -233,27 +218,24 @@
         slots[pl.ds(pl.multiple_of(p * 32 + m * 8, 8), 8), :] = staged[m, p]
 
     def forward(j, step):
+        if step < 4:
+            wait_bytes(ring.at[j, step - 1], z_recv.at[j, step - 1])
+        else:
+            wait_bytes(ring.at[j, 3, 0], z_recv.at[j, 3])
         for way in range(2):
-            def take(way=way):
-                hop(j, way, step - 1, partial.at[j, block(0)]).wait_recv()
-
             def send(way=way):
-                ring[j, way, step - 1] += partial[j, block(dest(j, way, step)), :]
-                hop(j, way, step, ring.at[j, way, step - 1]).start()
+                ring[j, step - 1, way] += partial[j, block(dest(j, way, step)), :]
+                hop(j, way, step, ring.at[j, step - 1, way]).start()
 
             if step <= 2:
-                take()
                 send()
             elif step == 3:
-                take()
                 pl.when(reach(j, way) == 4)(send)
-            else:
-                pl.when(reach(j, way) == 4)(take)
 
     def finish(j):
         done = partial[j, block(z), :]
         for way in range(2):
-            done = done + ring[j, way, reach(j, way) - 1]
+            done = done + ring[j, reach(j, way) - 1, way]
         m = j // 2
         for odd in range(2):
 
@@ -309,8 +291,7 @@
         )
 
     def wait_all(ref, count, sem):
-        whole = ref.at[pl.ds(0, count * 8)]
-        pltpu.make_async_copy(whole, whole, sem).wait()
+        wait_bytes(ref.at[pl.ds(0, count * 8)], sem)
 
     pl.semaphore_wait(ready, GROUPS - 1)
     for k in FAR_FIRST:
@@ -318,24 +299,11 @@
     part_in[rows(holder), :] = local[rows(holder), :]
     send_pair(CHUNKS // 2 - 1)
 
-    def gone(j, carry):
-        for k in range(1, PEERS):
-            y_copy(j, k).wait_send()
-        for way in range(2):
-            for step in range(3):
-                hop(j, way, step, ring.at[j, way, step]).wait_send()
-
-            @pl.when(reach(j, way) == 4)
-            def _(way=way):
-                hop(j, way, 3, ring.at[j, way, 2]).wait_send()
-        return carry
-
-    lax.fori_loop(0, CHUNKS, gone, 0)
-
-    for m in range(CHUNKS // 2):
-        for k in range(1, PEERS):
-            delivered(m, k).wait_recv()
-            deliver(m, k).wait_send()
+    wait_bytes(held.at[pl.ds(0, PEERS - 1)], y_send)
+    wait_bytes(partial.at[pl.ds(0, PLANES - 1)], z_send)
+
+    wait_bytes(slots.at[pl.ds(0, (PEERS - 1) * 32)], d_recv)
+    wait_bytes(slots.at[pl.ds(0, (PEERS - 1) * 32)], d_send)
     value = slots[...]
     first, rest = split2(value)
     second, third = split2(value - first.astype(F32))
@@ -376,7 +344,7 @@
             pltpu.VMEM((CHUNKS, 256, 256), BF16),
             pltpu.VMEM((CHUNKS, 256, 256), F32),
             pltpu.VMEM((CHUNKS, 256, 256), F32),
-            pltpu.VMEM((CHUNKS, 2, 4, 32, 256), F32),
+            pltpu.VMEM((CHUNKS, 4, 2, 32, 256), F32),
             pltpu.VMEM((BLOCKS, 128), F32),
             pltpu.VMEM((BLOCKS, 128), jnp.int32),
             pltpu.VMEM((256, 128), F32),
@@ -388,9 +356,9 @@
             pltpu.VMEM((PLANES * 8, 256), F32),
             dma((4,)),
             pltpu.SemaphoreType.REGULAR,
-            dma((CHUNKS, PEERS)), dma((CHUNKS, PEERS)),
-            dma((CHUNKS, 2, 4)), dma((CHUNKS, 2, 4)),
-            dma((CHUNKS // 2, PEERS)), dma((CHUNKS // 2, PEERS)),
+            dma, dma((CHUNKS,)),
+            dma, dma((CHUNKS, 4)),
+            dma, dma,
             dma, dma, dma, dma, dma, dma,
         ],
         compiler_params=pltpu.CompilerParams(

time: 71.1 us -> 68.7 us (0.966)
  Pallas kernels: 68.2 us -> 65.7 us
    pallas_call x1, Pallas kernels: 68.2 us -> 65.7 us  [shards(): pl.pallas_call(functools.partial(kernel, 1.0 / math.sqrt(slab), 1.0 / (sl...]
where the time goes in v3:
time: 68.7 us; the launch traced here: 68.5 us
  Pallas kernels  65.7 us (96%)
  local copies, waits for them, and re-layouts  1.36 us (2%)
  other arithmetic  0.78 us (1%)
    pallas_call x1, Pallas kernels, shards(): pl.pallas_call(functools.partial(kernel, 1.0 / math.sqrt(slab), 1.0 / (sl...  65.7 us

profile of v3, /device:TPU:1, one launch (start us, length us, event | category | flops | bytes accessed | tf_op | source)
XLA Modules:
  0.0 68.5 jit_solution(1158274226656236850)
XLA Ops:
  0.6 0.8 %pad_add_fusion.small = s32[80,128]{1,0:T(8,128)S(1)} fusion(s32[16,128]{1,0:T(8,128)} %bitcast.4, s32[64,128]{1,0:T(8,128)} %bitcast.3), kind=kLoop, calls=%fused_computation | loop fusion | flops 10240 | bytes 81920 | tf_op jit(solution)/shard_map/concatenate | solution.py:331
  1.4 65.7 %shard_map.50 = (f32[128,256]{1,0:T(8,128)S(1)}, f32[256,256]{1,0:T(8,128)S(1)}) custom-call(f32[8,256,256]{2,1,0:T(8,128)} %bitcast.5, s32[80,128]{1,0:T(8,128)S(1)} %pad_add_fusion.small), custom_call_target="tpu_custom_call" | custom-call | flops 2000000000 | bytes 4194304 | tf_op jit(solution)/shard_map/pallas_call | solution.py:333
  67.2 0.7 copy.7
  67.8 0.7 %copy.8 = f32[256,256]{1,0:T(8,128)} copy(f32[256,256]{1,0:T(8,128)S(1)} %get-tuple-element.5) | data formatting | bytes 524288

commit v4 on v3

--- a/solution.py
+++ b/solution.py
@@ -77,12 +77,11 @@
     for load in loads:
         load.start()
 
+    z_next = [(g, (z + k) % PLANES * PEERS + p) for k in (1, PLANES - 1)]
+    x_next = [((g + k) % GROUPS, dev) for k in (1, GROUPS - 1)]
     barrier = pltpu.get_barrier_semaphore()
-    for k in range(1, PLANES):
-        pl.semaphore_signal(barrier, inc=1, device_id=(g, z * PEERS + (p ^ k)), device_id_type=MESH)
-        pl.semaphore_signal(barrier, inc=1, device_id=(g, (z ^ k) * PEERS + p), device_id_type=MESH)
-    for k in range(1, GROUPS):
-        pl.semaphore_signal(barrier, inc=1, device_id=(g ^ k, dev), device_id_type=MESH)
+    for peer in [(g, z * PEERS + (p ^ k)) for k in (4, 5, 2, 3, 6, 7, 1)] + z_next + x_next:
+        pl.semaphore_signal(barrier, inc=1, device_id=peer, device_id_type=MESH)
 
     lane = lax.broadcasted_iota(jnp.int32, (128, 128), 1)
     row = lax.broadcasted_iota(jnp.int32, (128, 128), 0)
@@ -132,7 +131,7 @@
 
         @pl.when(j == 0)
         def _():
-            pl.semaphore_wait(barrier, PEERS - 1 + PLANES - 1 + GROUPS - 1)
+            pl.semaphore_wait(barrier, PEERS - 1 + 2 + 2)
 
         for k in (4, 5, 2, 3, 6, 7, 1):
             y_copy(j, k).start()
@@ -142,8 +141,11 @@
 
     lax.fori_loop(0, CHUNKS, low_bits, 0)
 
-    for k in range(1, GROUPS):
-        pl.semaphore_signal(ready, inc=1, device_id=(g ^ k, dev), device_id_type=MESH)
+    for stage in range(2):
+        for peer in x_next:
+            pl.semaphore_signal(ready.at[stage], inc=1, device_id=peer, device_id_type=MESH)
+        if stage == 0:
+            pl.semaphore_wait(ready.at[0], 2)
 
     before = (row < lane).astype(BF16)
 
@@ -252,10 +254,6 @@
             send_pair(m)
 
     def turn(t, carry):
-        @pl.when(t < CHUNKS)
-        def _():
-            produce(t)
-
         for step in range(1, 5):
             j = t - LAG * step
 
@@ -265,6 +263,10 @@
                 if step == 4:
                     finish(j)
 
+        @pl.when(t < CHUNKS)
+        def _():
+            produce(t)
+
         return carry
 
     lax.fori_loop(0, CHUNKS + 4 * LAG, turn, 0)
@@ -293,7 +295,7 @@
     def wait_all(ref, count, sem):
         wait_bytes(ref.at[pl.ds(0, count * 8)], sem)
 
-    pl.semaphore_wait(ready, GROUPS - 1)
+    pl.semaphore_wait(ready.at[1], 2)
     for k in FAR_FIRST:
         copy_a(k).start()
     part_in[rows(holder), :] = local[rows(holder), :]
@@ -355,7 +357,7 @@
             pltpu.VMEM((HOLDERS * 8, 256), F32),
             pltpu.VMEM((PLANES * 8, 256), F32),
             dma((4,)),
-            pltpu.SemaphoreType.REGULAR,
+            pltpu.SemaphoreType.REGULAR((2,)),
             dma, dma((CHUNKS,)),
             dma, dma((CHUNKS, 4)),
             dma, dma,

time: 68.7 us -> 67 us (0.975)
  Pallas kernels: 65.7 us -> 64.1 us
    pallas_call x1, Pallas kernels: 65.7 us -> 64.1 us  [shards(): pl.pallas_call(functools.partial(kernel, 1.0 / math.sqrt(slab), 1.0 / (sl...]
where the time goes in v4:
time: 67 us; the launch traced here: 66.9 us
  Pallas kernels  64.1 us (96%)
  local copies, waits for them, and re-layouts  1.36 us (2%)
  other arithmetic  0.78 us (1%)
    pallas_call x1, Pallas kernels, shards(): pl.pallas_call(functools.partial(kernel, 1.0 / math.sqrt(slab), 1.0 / (sl...  64.1 us
    unnamed x2, local copies, waits for them, and re-layouts  1.36 us

profile of v4, /device:TPU:1, one launch (start us, length us, event | category | flops | bytes accessed | tf_op | source)
XLA Modules:
  0.0 66.9 jit_solution(5691054617309080916)
XLA Ops:
  0.6 0.8 %pad_add_fusion.small = s32[80,128]{1,0:T(8,128)S(1)} fusion(s32[16,128]{1,0:T(8,128)} %bitcast.4, s32[64,128]{1,0:T(8,128)} %bitcast.3), kind=kLoop, calls=%fused_computation | loop fusion | flops 10240 | bytes 81920 | tf_op jit(solution)/shard_map/concatenate | solution.py:333
  1.4 64.1 %shard_map.50 = (f32[128,256]{1,0:T(8,128)S(1)}, f32[256,256]{1,0:T(8,128)S(1)}) custom-call(f32[8,256,256]{2,1,0:T(8,128)} %bitcast.5, s32[80,128]{1,0:T(8,128)S(1)} %pad_add_fusion.small), custom_call_target="tpu_custom_call" | custom-call | flops 2000000000 | bytes 4194304 | tf_op jit(solution)/shard_map/pallas_call | solution.py:335
  65.5 0.7 copy.7
  66.2 0.7 %copy.8 = f32[256,256]{1,0:T(8,128)} copy(f32[256,256]{1,0:T(8,128)S(1)} %get-tuple-element.5) | data formatting | bytes 524288

commit v5 on v4

v5 whole, which is shorter than its diff:
```python
import functools
import math

import jax
import jax.numpy as jnp
from jax import lax
from jax.experimental import pallas as pl
from jax.experimental.pallas import tpu as pltpu
from jax.sharding import PartitionSpec as P

MESH = pl.DeviceIdType.MESH
F32 = jnp.float32
BF16 = jnp.bfloat16

GROUPS = 4
PLANES = 8
PEERS = 8
CHUNKS = 8
UNITS = 2 * CHUNKS
IN_RANGE = 32
SLOTS = 4
BLOCKS = 64
HOLDERS = 32
FAR_FIRST = tuple(k ^ 20 for k in range(HOLDERS) if k != 20)
LAG = 4


def butterfly(parts):
    span = 1
    while span < len(parts):
        out = list(parts)
        for a in range(len(parts)):
            if a & span == 0:
                out[a] = parts[a] + parts[a + span]
                out[a + span] = parts[a] - parts[a + span]
        parts = out
        span *= 2
    return parts


def split2(value):
    high = value.astype(BF16)
    return high, (value - high.astype(F32)).astype(BF16)


def dot(a, b):
    return jnp.dot(a, b, preferred_element_type=F32)


def dot_first(a, b):
    return lax.dot_general(a, b, (((0,), (0,)), ((), ())), preferred_element_type=F32)


def kernel(
    scale, gram_scale,
    design, samples_in, bits_in, sketch, gram,
    small,    held, signs, table, arrived, partial, ring, code, owner, code_wide, pick,
    staged, slots, local, part_in, z_in,
    load_sem, ready, y_send, y_recv, z_send, z_recv, d_send, d_recv,
    a_send, a_recv, b_send, b_recv, c_send, c_recv,
):
    g = lax.axis_index("grp")
    dev = lax.axis_index("dev")
    z = dev >> 3
    p = dev & 7
    holder = g * PEERS + p

    def holder_id(k):
        return (g ^ (k >> 3), dev ^ (k & 7))

    loads = [
        pltpu.make_async_copy(
            design.at[:, pl.ds(i * 64, 64), pl.ds(half * 128, 128)],
            held.at[:, half, pl.ds(i * 64, 64)],
            load_sem.at[2 * i + half],
        )
        for i in range(4)
        for half in range(2)
    ]
    small_loads = [
        pltpu.make_async_copy(bits_in, small.at[pl.ds(BLOCKS, 16)], load_sem.at[8]),
        pltpu.make_async_copy(samples_in, small.at[pl.ds(0, BLOCKS)], load_sem.at[9]),
    ]
    for load in small_loads + loads:
        load.start()

    z_next = [(g, (dev + k * PEERS) & 63) for k in (1, PLANES - 1)]
    x_next = [((g + k) & (GROUPS - 1), dev) for k in (1, GROUPS - 1)]
    barrier = pltpu.get_barrier_semaphore()
    for peer in [(g, dev ^ k) for k in (4, 5, 2, 3, 6, 7, 1)] + z_next + x_next:
        pl.semaphore_signal(barrier, inc=1, device_id=peer, device_id_type=MESH)

    for load in small_loads:
        load.wait()

    lane = lax.broadcasted_iota(jnp.int32, (128, 128), 1)
    row = lax.broadcasted_iota(jnp.int32, (128, 128), 0)
    ones = jnp.ones((128, 128), BF16)
    for i in range(16):
        sign = (2 * small[pl.ds(BLOCKS + i, 1), :] - 1).astype(F32)
        diagonal = jnp.where(lane == row, jnp.broadcast_to(sign, (128, 128)), 0.0)
        signs[pl.ds(i * 128, 128), :] = dot(diagonal.astype(BF16), ones)

    target = small[pl.ds(0, BLOCKS), :]
    owner[...] = (target >> 5) & 63
    along_z = (target >> 14) & z
    flip = (along_z ^ (along_z >> 1) ^ (along_z >> 2)) & 1
    code[...] = ((((target >> 11) & 7) << 5) | (target & 31) | (flip << 8) | 512).astype(F32)

    for i in range(8):
        part = pl.ds(i * IN_RANGE, IN_RANGE)
        for half in range(2):
            if i % 2 == 0:
                loads[i + half].wait()
            parts = [held[k, half, part, :] * signs[pl.ds(k * 256 + i * IN_RANGE, IN_RANGE), :] for k in range(8)]
            for k, value in enumerate(butterfly(parts)):
                held[k, half, part, :] = value

    def y_copy(u, k):
        peer = p ^ k
        return pltpu.make_async_remote_copy(
            held.at[u >> 1, u & 1, pl.ds(pl.multiple_of(peer * IN_RANGE, IN_RANGE), IN_RANGE)],
            arrived.at[u, pl.ds(pl.multiple_of(p * IN_RANGE, IN_RANGE), IN_RANGE)],
            y_send, y_recv.at[u],
            device_id=(g, dev ^ k), device_id_type=MESH,
        )

    def wait_bytes(ref, sem):
        pltpu.make_async_copy(ref, ref, sem).wait()

    def low_bits(u, carry):
        parts = [held[u >> 1, u & 1, pl.ds(k * IN_RANGE, IN_RANGE), :] for k in range(8)]
        for k, value in enumerate(butterfly(parts)):
            held[u >> 1, u & 1, pl.ds(k * IN_RANGE, IN_RANGE), :] = value

        @pl.when(u == 0)
        def _():
            pl.semaphore_wait(barrier, PEERS - 1 + 2 + 2)

        for k in (4, 5, 2, 3, 6, 7, 1):
            y_copy(u, k).start()
        mine = pl.multiple_of(p * IN_RANGE, IN_RANGE)
        arrived[u, pl.ds(mine, IN_RANGE), :] = held[u >> 1, u & 1, pl.ds(mine, IN_RANGE), :]
        return carry

    lax.fori_loop(0, UNITS, low_bits, 0)

    for stage in range(2):
        for peer in x_next:
            pl.semaphore_signal(ready.at[stage], inc=1, device_id=peer, device_id_type=MESH)
        if stage == 0:
            pl.semaphore_wait(ready.at[0], 2)

    before = (row < lane).astype(BF16)

    def build(j, carry):
        here = owner[...] == 8 * j + p
        rank = dot(here.astype(F32).astype(BF16), before)
        for i in range(SLOTS):
            chosen = jnp.where(here & (rank == float(i)), code[...], 0.0)
            column = jnp.sum(chosen, axis=1, keepdims=True)
            code_wide[pl.ds(i, BLOCKS, stride=SLOTS), :] = jnp.broadcast_to(column, (BLOCKS, 128))
        wide = code_wide[...].astype(jnp.int32)
        at = lax.broadcasted_iota(jnp.int32, (256, 128), 1) + 256
        for half in range(2):
            v = wide & (at + 128 * half)
            v = v ^ (v >> 8)
            v = v ^ (v >> 4)
            v = v ^ (v >> 2)
            v = v ^ (v >> 1)
            value = jnp.where(wide >= 512, 1 - 2 * (v & 1), 0).astype(F32)
            table[j, :, pl.ds(half * 128, 128)] = value.astype(BF16)
        return carry

    lax.fori_loop(0, CHUNKS, build, 0)

    own = jnp.broadcast_to((small[pl.ds(dev, 1), :] >> 5) & 63, (128, 128)).astype(F32)
    same = jnp.where((own == own.T) & (row < lane), 1.0, 0.0)
    rank = jnp.broadcast_to(jnp.sum(same, axis=0, keepdims=True), (128, 128))
    own = own.astype(jnp.int32)
    place = ((own & 7) * 32 + (own >> 3) * 4).astype(F32) + rank
    place = place.T
    for half in range(2):
        at = (lane + 128 * half).astype(F32)
        pick[:, pl.ds(half * 128, 128)] = jnp.where(place == at, 1.0, 0.0).astype(BF16)

    local[...] = jnp.zeros_like(local)

    def block(index):
        return pl.ds(pl.multiple_of(index * 32, 32), 32)

    def hop(u, way, step, source):
        return pltpu.make_async_remote_copy(
            source, ring.at[u, step, way], z_send, z_recv.at[u, step],
            device_id=z_next[way], device_id_type=MESH,
        )

    def reach(u, way):
        return 3 + ((u + way + 1) & 1)

    def dest(u, way, step):
        far = reach(u, way) - step
        return (z + far) & 7 if way == 0 else (z - far) & 7

    def produce(u):
        wait_bytes(arrived.at[u, pl.ds(0, (PEERS - 1) * IN_RANGE)], y_recv.at[u])
        high, low = split2(arrived[u])
        partial[u] = dot(table[u >> 1], high) + dot(table[u >> 1], low)
        for way in range(2):
            hop(u, way, 0, partial.at[u, block(dest(u, way, 0))]).start()

    def deliver(m, k):
        peer = p ^ k
        return pltpu.make_async_remote_copy(
            staged.at[m, peer], slots.at[pl.ds(pl.multiple_of(p * 32 + m * 8, 8), 8)],
            d_send, d_recv,
            device_id=(g, dev ^ k), device_id_type=MESH,
        )

    def send_pair(m):
        for k in (4, 5, 2, 3, 6, 7, 1):
            deliver(m, k).start()
        slots[pl.ds(pl.multiple_of(p * 32 + m * 8, 8), 8), :] = staged[m, p]

    def forward(u, step):
        if step < 4:
            wait_bytes(ring.at[u, step - 1], z_recv.at[u, step - 1])
        else:
            wait_bytes(ring.at[u, 3, 0], z_recv.at[u, 3])
        for way in range(2):
            def send(way=way):
                ring[u, step - 1, way] += partial[u, block(dest(u, way, step)), :]
                hop(u, way, step, ring.at[u, step - 1, way]).start()

            if step <= 2:
                send()
            elif step == 3:
                pl.when(reach(u, way) == 4)(send)

    def finish(j):
        m = j >> 1
        halves = []
        for half in range(2):
            u = 2 * j + half
            done = partial[u, block(z), :]
            for way in range(2):
                done = done + ring[u, reach(u, way) - 1, way]
            halves.append(done)
        done = jnp.concatenate(halves, axis=1)
        high, low = split2(done)
        local[...] += dot_first(high, high) + dot_first(high, low) + dot_first(low, high)
        for odd in range(2):

            @pl.when((j & 1) == odd)
            def _(odd=odd):
                for k in range(PEERS):
                    staged[m, k, pl.ds(odd * SLOTS, SLOTS), :] = done[k * SLOTS : (k + 1) * SLOTS, :]

        @pl.when(((j & 1) == 1) & (j < CHUNKS - 1))
        def _():
            send_pair(m)

    def turn(t, carry):
        for step in range(1, 5):
            u = t - LAG * step

            @pl.when((u >= 0) & (u < UNITS))
            def _(u=u, step=step):
                forward(u, step)
                if step == 4:
                    pl.when((u & 1) == 1)(lambda: finish(u >> 1))

        @pl.when(t < UNITS)
        def _():
            produce(t)

        return carry

    lax.fori_loop(0, UNITS + 4 * LAG, turn, 0)

    def rows(index):
        return pl.ds(pl.multiple_of(index * 8, 8), 8)

    def copy_a(k):
        return pltpu.make_async_remote_copy(
            local.at[rows(holder ^ k)], part_in.at[rows(holder)], a_send, a_recv,
            device_id=holder_id(k), device_id_type=MESH,
        )

    def copy_b(k):
        return pltpu.make_async_remote_copy(
            z_in.at[rows(z)], z_in.at[rows(z)], b_send, b_recv,
            device_id=(g, dev ^ (k << 3)), device_id_type=MESH,
        )

    def copy_c(k):
        return pltpu.make_async_remote_copy(
            gram.at[rows(holder)], gram.at[rows(holder)], c_send, c_recv,
            device_id=holder_id(k), device_id_type=MESH,
        )

    def wait_all(ref, count, sem):
        wait_bytes(ref.at[pl.ds(0, count * 8)], sem)

    pl.semaphore_wait(ready.at[1], 2)
    for k in FAR_FIRST:
        copy_a(k).start()
    part_in[rows(holder), :] = local[rows(holder), :]
    wait_bytes(held.at[pl.ds(0, PEERS - 1)], y_send)
    wait_bytes(partial.at[pl.ds(0, 2 * (PLANES - 1))], z_send)

    wait_all(part_in, HOLDERS - 1, a_recv)
    z_in[rows(z), :] = jnp.sum(part_in[...].reshape(HOLDERS, 8, 256), axis=0)
    for k in (4, 3, 5, 2, 6, 1, 7):
        copy_b(k).start()
    send_pair(CHUNKS // 2 - 1)
    wait_all(part_in, HOLDERS - 1, a_send)
    wait_all(z_in, PLANES - 1, b_recv)
    gram[rows(holder), :] = jnp.sum(z_in[...].reshape(PLANES, 8, 256), axis=0) * gram_scale
    for k in FAR_FIRST:
        copy_c(k).start()
    wait_bytes(slots.at[pl.ds(0, (PEERS - 1) * 32)], d_recv)
    wait_bytes(slots.at[pl.ds(0, (PEERS - 1) * 32)], d_send)
    value = slots[...]
    first, rest = split2(value)
    second, third = split2(value - first.astype(F32))
    sketch[...] = (dot(pick[...], first) + dot(pick[...], second) + dot(pick[...], third)) * scale

    wait_all(z_in, PLANES - 1, b_send)
    wait_all(gram, HOLDERS - 1, c_recv)
    wait_all(gram, HOLDERS - 1, c_send)


def shards(design, sign_bits, sample_rows):
    rows, width = design.shape
    slab = rows * lax.axis_size("dev")
    total = lax.axis_size("grp") * sample_rows.shape[1]
    vmem = pl.BlockSpec(memory_space=pltpu.VMEM)
    hbm = pl.BlockSpec(memory_space=pltpu.HBM)
    operands = [
        pltpu.with_memory_space_constraint(x, pltpu.HBM)
        for x in (
            design.reshape(CHUNKS, 256, width),
            sample_rows.reshape(BLOCKS, 128),
            sign_bits.reshape(16, 128),
        )
    ]
    dma = pltpu.SemaphoreType.DMA
    return pl.pallas_call(
        functools.partial(kernel, 1.0 / math.sqrt(slab), 1.0 / (slab * total)),
        out_shape=(
            jax.ShapeDtypeStruct((128, width), F32),
            jax.ShapeDtypeStruct((width, width), F32),
        ),
        in_specs=[hbm, hbm, hbm],
        out_specs=(vmem, vmem),
        scratch_shapes=[
            pltpu.VMEM((BLOCKS + 16, 128), jnp.int32),
            pltpu.VMEM((CHUNKS, 2, 256, 128), F32),
            pltpu.VMEM((2048, 128), F32),
            pltpu.VMEM((CHUNKS, 256, 256), BF16),
            pltpu.VMEM((UNITS, 256, 128), F32),
            pltpu.VMEM((UNITS, 256, 128), F32),
            pltpu.VMEM((UNITS, 4, 2, 32, 128), F32),
            pltpu.VMEM((BLOCKS, 128), F32),
            pltpu.VMEM((BLOCKS, 128), jnp.int32),
            pltpu.VMEM((256, 128), F32),
            pltpu.VMEM((128, 256), BF16),
            pltpu.VMEM((CHUNKS // 2, PEERS, 8, 256), F32),
            pltpu.VMEM((256, 256), F32),
            pltpu.VMEM((256, 256), F32),
            pltpu.VMEM((HOLDERS * 8, 256), F32),
            pltpu.VMEM((PLANES * 8, 256), F32),
            dma((10,)),
            pltpu.SemaphoreType.REGULAR((2,)),
            dma, dma((UNITS,)),
            dma, dma((UNITS, 4)),
            dma, dma,
            dma, dma, dma, dma, dma, dma,
        ],
        compiler_params=pltpu.CompilerParams(
            collective_id=0, has_side_effects=True, vmem_limit_bytes=52 << 20
        ),
        cost_estimate=pl.CostEstimate(flops=2 * 10**9, bytes_accessed=4 << 20, transcendentals=0),
    )(*operands)


def solution(mesh):
    return jax.shard_map(
        shards,
        mesh=mesh,
        in_specs=(P(("grp", "dev"), None), P(("grp", "dev")), P("grp", None)),
        out_specs=(P(("grp", "dev"), None), P()),
        check_vma=False,
    )
```

time: 67 us -> 66 us (0.985)
  other arithmetic: 0.78 us -> 0 us
    concatenate x1 -> x0, other arithmetic: 0.78 us -> none  [shards(): jnp.concatenate([sample_rows.reshape(BLOCKS, 128), sign_bits.reshape(16,...]
where the time goes in v5:
time: 66 us; the launch traced here: 65.8 us
  Pallas kernels  63.8 us (97%)
  local copies, waits for them, and re-layouts  1.36 us (2%)
    pallas_call x1, Pallas kernels, shards(): pl.pallas_call(functools.partial(kernel, 1.0 / math.sqrt(slab), 1.0 / (sl...  63.8 us
    unnamed x2, local copies, waits for them, and re-layouts  1.36 us

profile of v5, /device:TPU:1, one launch (start us, length us, event | category | flops | bytes accessed | tf_op | source)
XLA Modules:
  0.0 65.8 jit_solution(15022269063064349205)
XLA Ops:
  0.6 63.8 %shard_map.50 = (f32[128,256]{1,0:T(8,128)S(1)}, f32[256,256]{1,0:T(8,128)S(1)}) custom-call(f32[8,256,256]{2,1,0:T(8,128)} %bitcast.3, s32[64,128]{1,0:T(8,128)} %bitcast.4, s32[16,128]{1,0:T(8,128)} %bitcast.5), custom_call_target="tpu_custom_call" | custom-call | flops 2000000000 | bytes 4194304 | tf_op jit(solution)/shard_map/pallas_call | solution.py:349
  64.5 0.7 copy.7
  65.1 0.7 %copy.8 = f32[256,256]{1,0:T(8,128)} copy(f32[256,256]{1,0:T(8,128)S(1)} %get-tuple-element.5) | data formatting | bytes 524288

commit v6 on v5

--- a/solution.py
+++ b/solution.py
@@ -23,6 +23,11 @@
 HOLDERS = 32
 FAR_FIRST = tuple(k ^ 20 for k in range(HOLDERS) if k != 20)
 LAG = 4
+
+
+def hops(k):
+    along = (0, 1, 2, 1)
+    return 10 * (along[k >> 3] + along[(k >> 1) & 3]) + (k & 1)
 
 
 def butterfly(parts):
@@ -205,7 +210,8 @@
     def produce(u):
         wait_bytes(arrived.at[u, pl.ds(0, (PEERS - 1) * IN_RANGE)], y_recv.at[u])
         high, low = split2(arrived[u])
-        partial[u] = dot(table[u >> 1], high) + dot(table[u >> 1], low)
+        both = dot(table[u >> 1], jnp.concatenate([high, low], axis=1))
+        partial[u] = both[:, :128] + both[:, 128:]
         for way in range(2):
             hop(u, way, 0, partial.at[u, block(dest(u, way, 0))]).start()
 
@@ -248,7 +254,9 @@
             halves.append(done)
         done = jnp.concatenate(halves, axis=1)
         high, low = split2(done)
-        local[...] += dot_first(high, high) + dot_first(high, low) + dot_first(low, high)
+        local[...] += dot_first(
+            jnp.concatenate([high, high, low], axis=0), jnp.concatenate([high, low, high], axis=0)
+        )
         for odd in range(2):
 
             @pl.when((j & 1) == odd)
@@ -303,7 +311,7 @@
         wait_bytes(ref.at[pl.ds(0, count * 8)], sem)
 
     pl.semaphore_wait(ready.at[1], 2)
-    for k in FAR_FIRST:
+    for k in sorted(FAR_FIRST, key=hops, reverse=True):
         copy_a(k).start()
     part_in[rows(holder), :] = local[rows(holder), :]
     wait_bytes(held.at[pl.ds(0, PEERS - 1)], y_send)
@@ -317,7 +325,7 @@
     wait_all(part_in, HOLDERS - 1, a_send)
     wait_all(z_in, PLANES - 1, b_recv)
     gram[rows(holder), :] = jnp.sum(z_in[...].reshape(PLANES, 8, 256), axis=0) * gram_scale
-    for k in FAR_FIRST:
+    for k in sorted(FAR_FIRST, key=hops, reverse=True):
         copy_c(k).start()
     wait_bytes(slots.at[pl.ds(0, (PEERS - 1) * 32)], d_recv)
     wait_bytes(slots.at[pl.ds(0, (PEERS - 1) * 32)], d_send)

time: 66 us -> 65.5 us (level)
  no operation moved by 1% of the time
where the time goes in v6:
time: 65.5 us; the launch traced here: 65.3 us
  Pallas kernels  63.3 us (97%)
  local copies, waits for them, and re-layouts  1.36 us (2%)
    pallas_call x1, Pallas kernels, shards(): pl.pallas_call(functools.partial(kernel, 1.0 / math.sqrt(slab), 1.0 / (sl...  63.3 us
    unnamed x2, local copies, waits for them, and re-layouts  1.36 us

profile of v6, /device:TPU:1, one launch (start us, length us, event | category | flops | bytes accessed | tf_op | source)
XLA Modules:
  0.0 65.3 jit_solution(7215738767669982301)
XLA Ops:
  0.6 63.3 %shard_map.50 = (f32[128,256]{1,0:T(8,128)S(1)}, f32[256,256]{1,0:T(8,128)S(1)}) custom-call(f32[8,256,256]{2,1,0:T(8,128)} %bitcast.3, s32[64,128]{1,0:T(8,128)} %bitcast.4, s32[16,128]{1,0:T(8,128)} %bitcast.5), custom_call_target="tpu_custom_call" | custom-call | flops 2000000000 | bytes 4194304 | tf_op jit(solution)/shard_map/pallas_call | solution.py:357
  64.0 0.7 %copy.7 = f32[128,256]{1,0:T(8,128)} copy(f32[128,256]{1,0:T(8,128)S(1)} %get-tuple-element.4) | data formatting | bytes 262144
  64.6 0.7 %copy.8 = f32[256,256]{1,0:T(8,128)} copy(f32[256,256]{1,0:T(8,128)S(1)} %get-tuple-element.5) | data formatting | bytes 524288

commit v7 on v6

--- a/solution.py
+++ b/solution.py
@@ -86,14 +86,14 @@
         pltpu.make_async_copy(bits_in, small.at[pl.ds(BLOCKS, 16)], load_sem.at[8]),
         pltpu.make_async_copy(samples_in, small.at[pl.ds(0, BLOCKS)], load_sem.at[9]),
     ]
-    for load in small_loads + loads:
-        load.start()
 
     z_next = [(g, (dev + k * PEERS) & 63) for k in (1, PLANES - 1)]
     x_next = [((g + k) & (GROUPS - 1), dev) for k in (1, GROUPS - 1)]
     barrier = pltpu.get_barrier_semaphore()
     for peer in [(g, dev ^ k) for k in (4, 5, 2, 3, 6, 7, 1)] + z_next + x_next:
         pl.semaphore_signal(barrier, inc=1, device_id=peer, device_id_type=MESH)
+    for load in small_loads + loads:
+        load.start()
 
     for load in small_loads:
         load.wait()

time: 65.5 us -> 65.4 us (level)
  no operation moved by 1% of the time
where the time goes in v7:
time: 65.4 us; the launch traced here: 65.3 us
  Pallas kernels  63.3 us (97%)
  local copies, waits for them, and re-layouts  1.36 us (2%)
    pallas_call x1, Pallas kernels, shards(): pl.pallas_call(functools.partial(kernel, 1.0 / math.sqrt(slab), 1.0 / (sl...  63.3 us
    unnamed x2, local copies, waits for them, and re-layouts  1.36 us

profile of v7, /device:TPU:1, one launch (start us, length us, event | category | flops | bytes accessed | tf_op | source)
XLA Modules:
  0.0 65.3 jit_solution(2161487502264014457)
XLA Ops:
  0.6 63.3 %shard_map.50 = (f32[128,256]{1,0:T(8,128)S(1)}, f32[256,256]{1,0:T(8,128)S(1)}) custom-call(f32[8,256,256]{2,1,0:T(8,128)} %bitcast.3, s32[64,128]{1,0:T(8,128)} %bitcast.4, s32[16,128]{1,0:T(8,128)} %bitcast.5), custom_call_target="tpu_custom_call" | custom-call | flops 2000000000 | bytes 4194304 | tf_op jit(solution)/shard_map/pallas_call | solution.py:357
  64.0 0.7 %copy.7 = f32[128,256]{1,0:T(8,128)} copy(f32[128,256]{1,0:T(8,128)S(1)} %get-tuple-element.4) | data formatting | bytes 262144
  64.6 0.7 %copy.8 = f32[256,256]{1,0:T(8,128)} copy(f32[256,256]{1,0:T(8,128)S(1)} %get-tuple-element.5) | data formatting | bytes 524288
